TPU v7x, 256 devices: a whole 4x4x8 slice. The times are simulated.
256 devices in a mesh: wide: 32 (over x, z), narrow: 8 (over y, core).
Axes of the slice: x: 4, y: 4, z: 8, core: 2. Of those that a mesh axis runs over, the one named last changes fastest.
Arguments:
- hidden: bfloat16 [2, 2048, 8192], P(None, 'wide', 'narrow'), may hold values from -6 to 6
- router_weight: float32 [8192], P('narrow'), may hold values from -0.0625 to 0.0625
- teacher: float32 [2, 2048], P(None, 'wide'), may hold values from 0.05 to 0.95
- positions: int32 [2, 256], replicated, may hold values from 0 to 2047, as said below
- cotangent: bfloat16 [2, 256, 8192], P(None, 'wide', 'narrow'), may hold values from -6 to 6
- gate_weight: bfloat16 [8192, 28672], P('narrow', 'wide'), may hold values from -0.0625 to 0.0625
- up_weight: bfloat16 [8192, 28672], P('narrow', 'wide'), may hold values from -0.0625 to 0.0625
- down_weight: bfloat16 [28672, 8192], P('wide', 'narrow'), may hold values from -0.03125 to 0.03125
Outputs:
- hidden_grad: bfloat16 [2, 2048, 8192], P(None, 'wide', 'narrow')
- router_grad: float32 [8192], P('narrow')
- gate_grad: bfloat16 [8192, 28672], P('narrow', 'wide')
- up_grad: bfloat16 [8192, 28672], P('narrow', 'wide')
- down_grad: bfloat16 [28672, 8192], P('wide', 'narrow')
Inputs may be any that keep to these rules, and one draw needn't show every extreme that they name: In each slab the positions rise strictly, and every aligned block of 64 slab positions holds exactly 8 of them.
All inputs are finite; a program needn't handle non-finite values.
Results may differ from a plain program's by a relative error of at most 0.0058.
Values may be sent and summed in bfloat16 or wider, within the bound.
A program may use at most 64 MiB of HBM per device.

v0:
```python
import jax
import jax.numpy as jnp
from jax import lax
from jax.sharding import PartitionSpec as P


def gating(gate, up):
    sig = jax.nn.sigmoid(gate)
    return (sig, (gate * sig * up).astype(jnp.bfloat16))


def pre_grads(act_grad, gate, up):
    sig = jax.nn.sigmoid(gate)
    gate_pre = (act_grad * up * sig * (1.0 + gate * (1.0 - sig))).astype(jnp.bfloat16)
    up_pre = (act_grad * gate * sig).astype(jnp.bfloat16)
    return (gate_pre, up_pre)


def on_device(
    hidden, router_weight, teacher, positions, cotangent, gate_weight, up_weight, down_weight
):
    slabs, rows_dev, width = hidden.shape
    wide_count = lax.axis_size("wide")
    wide_index = lax.axis_index("wide")
    routed_dev = positions.shape[1] // wide_count
    hidden32 = hidden.reshape(-1, width).astype(jnp.float32)
    logit_part = jnp.dot(hidden32, router_weight, precision=lax.Precision.HIGHEST)
    logits = lax.psum(logit_part, "narrow").reshape(slabs, rows_dev)
    slab_index = jnp.arange(slabs, dtype=jnp.int32)[:, None]
    local_pos = (
        lax.dynamic_slice_in_dim(positions, wide_index * routed_dev, routed_dev, 1)
        - wide_index * rows_dev
    )
    scale = jax.nn.sigmoid(logits[slab_index, local_pos])
    cot32 = cotangent.astype(jnp.float32)
    out_grad = (scale[:, :, None] * cot32).astype(jnp.bfloat16).reshape(-1, width)
    whole_slab = lax.all_gather(hidden, "wide", axis=1, tiled=True)
    order = positions.reshape(slabs, wide_count, routed_dev).transpose(1, 0, 2)
    slab_ids = jnp.broadcast_to(jnp.arange(slabs, dtype=jnp.int32)[None, :, None], order.shape)
    rows = whole_slab[slab_ids, order].reshape(-1, width)
    gate_part = jnp.dot(rows, gate_weight, preferred_element_type=jnp.float32)
    up_part = jnp.dot(rows, up_weight, preferred_element_type=jnp.float32)
    gate, up = lax.psum((gate_part, up_part), "narrow")
    sig, act = gating(gate, up)
    mlp_out = lax.psum_scatter(
        jnp.dot(act, down_weight, preferred_element_type=jnp.float32),
        "wide",
        scatter_dimension=0,
        tiled=True,
    )
    dot_part = jnp.sum(cot32 * mlp_out.reshape(cot32.shape), axis=-1)
    dots = lax.psum(dot_part, "narrow")
    out_all = lax.all_gather(out_grad, "wide", axis=0, tiled=True)
    down_grad = lax.dot_general(
        act, out_all, (((0,), (0,)), ((), ())), preferred_element_type=jnp.float32
    ).astype(jnp.bfloat16)
    act_part = lax.dot_general(
        out_all, down_weight, (((1,), (1,)), ((), ())), preferred_element_type=jnp.float32
    )
    act_grad = lax.psum(act_part, "narrow")
    gate_pre, up_pre = pre_grads(act_grad, gate, up)
    gate_grad = lax.dot_general(
        rows, gate_pre, (((0,), (0,)), ((), ())), preferred_element_type=jnp.float32
    ).astype(jnp.bfloat16)
    up_grad = lax.dot_general(
        rows, up_pre, (((0,), (0,)), ((), ())), preferred_element_type=jnp.float32
    ).astype(jnp.bfloat16)
    first = lax.dot_general(
        gate_pre, gate_weight, (((1,), (1,)), ((), ())), preferred_element_type=jnp.float32
    )
    second = lax.dot_general(
        up_pre, up_weight, (((1,), (1,)), ((), ())), preferred_element_type=jnp.float32
    )
    rows_grad = lax.psum_scatter(first + second, "wide", scatter_dimension=0, tiled=True)
    logit_grad = jax.nn.sigmoid(logits) - teacher
    logit_grad = logit_grad.at[slab_index, local_pos].add(scale * (1.0 - scale) * dots)
    hidden_grad = logit_grad[:, :, None] * router_weight[None, None, :]
    hidden_grad = hidden_grad.at[slab_index, local_pos].add(rows_grad.reshape(cot32.shape))
    router_part = jnp.dot(logit_grad.reshape(-1), hidden32, precision=lax.Precision.HIGHEST)
    router_grad = lax.psum(router_part, "wide")
    return (hidden_grad.astype(jnp.bfloat16), router_grad, gate_grad, up_grad, down_grad)


def solution(mesh):
    in_specs = (
        P(None, "wide", "narrow"),
        P("narrow"),
        P(None, "wide"),
        P(),
        P(None, "wide", "narrow"),
        P("narrow", "wide"),
        P("narrow", "wide"),
        P("wide", "narrow"),
    )
    out_specs = (
        P(None, "wide", "narrow"),
        P("narrow"),
        P("narrow", "wide"),
        P("narrow", "wide"),
        P("wide", "narrow"),
    )
    return jax.shard_map(
        on_device, mesh=mesh, in_specs=in_specs, out_specs=out_specs, check_vma=False
    )
```

profile of v0, /device:TPU:8, one launch (start us, length us, event | category | flops | bytes accessed | tf_op | source)
XLA Modules:
  0.0 815.2 jit_solution(4886967882469046980)
XLA Ops:
  8.9 102.9 %all-gather.3.cloned.1.call-done = bf16[2,2048,1024]{2,1,0:T(8,128)(2,1)} async-done(((bf16[2,64,1024]{2,1,0:T(8,128)(2,1)}), bf16[2,2048,1024]{2,1,0:T(8,128)(2,1)}) %all-gather.3.cloned.1.call-update) | async-done | bytes 8388624 | tf_op jit(solution)/shard_map/all_gather | solution.py:37
  111.8 7.8 gather_fusion.1
  119.7 4.4 fusion.11
  124.1 2.5 fusion.12
  126.6 70.7 %all-reduce.7.cloned.1.call-done = (f32[512,896]{1,0:T(8,128)}, f32[512,896]{1,0:T(8,128)}) async-done(((f32[512,896]{1,0:T(8,128)}, f32[512,896]{1,0:T(8,128)}), (f32[512,896]{1,0:T(8,128)}, f32[512,896]{1,0:T(8,128)})) %all-reduce.7.cloned.1.call-update) | async-done | bytes 3670032 | tf_op jit(solution)/shard_map/psum | solution.py:43
  197.3 2.6 multiply_convert_fusion.2
  199.9 0.9 copy-done.6
  200.8 2.6 fusion.13
  204.9 217.6 %reduce-scatter.3.cloned.1.call-done = f32[16,1024]{1,0:T(8,128)} async-done(((f32[512,1024]{1,0:T(8,128)}), f32[16,1024]{1,0:T(8,128)}) %reduce-scatter.3.cloned.1.call-update) | async-done | bytes 65552 | tf_op jit(solution)/shard_map/reduce_scatter | solution.py:45
  422.6 0.9 fusion
  423.5 10.0 %all-reduce = (f32[2,64]{1,0:T(2,128)S(1)}, f32[2,8]{1,0:T(2,128)S(1)}) all-reduce(f32[2,64]{1,0:T(2,128)S(1)} %reshape.43, f32[2,8]{1,0:T(2,128)S(1)} %fusion), channel_id=1, replica_groups=mesh['wide'=32,'narrow'=8] {'narrow'}, use_global_device_ids=true, to_apply=%region_0.0 | all-reduce | flops 144 | bytes 1152 | tf_op jit(solution)/shard_map/psum | solution.py:28
  435.0 74.6 %all-gather.5.cloned.1.call-done = bf16[512,1024]{1,0:T(8,128)(2,1)} async-done(((bf16[16,1024]{1,0:T(8,128)(2,1)}), bf16[512,1024]{1,0:T(8,128)(2,1)}) %all-gather.5.cloned.1.call-update) | async-done | bytes 1048592 | tf_op jit(solution)/shard_map/all_gather | solution.py:53
  509.7 3.7 fusion.14
  513.5 65.5 %all-reduce.5.cloned.1.call-done = f32[512,896]{1,0:T(8,128)} async-done(((f32[512,896]{1,0:T(8,128)}), f32[512,896]{1,0:T(8,128)}) %all-reduce.5.cloned.1.call-update) | async-done | bytes 1835024 | tf_op jit(solution)/shard_map/psum | solution.py:60
  579.0 3.6 multiply_convert_fusion
  582.6 1.3 fusion.15
  584.4 2.6 convolution_add_fusion
  587.8 1.3 scatter_fusion
  589.3 75.8 %psum.47 = f32[1024]{0:T(1024)} all-reduce(f32[1024]{0:T(1024)S(1)} %bitcast.57), channel_id=1, replica_groups=mesh['wide'=32,'narrow'=8] {'wide'}, use_global_device_ids=true, to_apply=%region_10.0 | all-reduce | flops 1024 | bytes 8192 | tf_op jit(solution)/shard_map/psum | solution.py:80
  665.3 4.0 convolution_convert_fusion
  669.3 2.5 convolution_convert_fusion.1
  671.8 2.5 convolution_convert_fusion.2
  674.4 131.1 %reduce-scatter.5.cloned.1.call-done = f32[16,1024]{1,0:T(8,128)} async-done(((f32[512,1024]{1,0:T(8,128)}), f32[16,1024]{1,0:T(8,128)}) %reduce-scatter.5.cloned.1.call-update) | async-done | bytes 65552 | tf_op jit(solution)/shard_map/reduce_scatter | solution.py:74
  805.5 2.1 scatter_fusion.1
  (58 shorter events, 7.2 us)
Async XLA Ops:
  7.2 193.6 %copy-start = (bf16[896,1024]{1,0:T(8,128)(2,1)S(1)}, bf16[896,1024]{1,0:T(8,128)(2,1)}, u32[]{:S(2)}) copy-start(bf16[896,1024]{1,0:T(8,128)(2,1)} %param.15) | copy-start | bytes 5505028
  7.2 104.6 %all-gather.3.cloned.1.call-start = ((), (), s32[]{:S(2)}) async-start(), calls=%async_computation.2 | async-start | bytes 8650752 | tf_op jit(solution)/shard_map/all_gather | solution.py:37
  7.9 189.4 %all-reduce.7.cloned.1.call-start = ((), (), s32[]{:S(2)}) async-start(), calls=%async_computation.7 | async-start | bytes 7340032 | tf_op jit(solution)/shard_map/psum | solution.py:43
  119.7 4.4 copy-start.2
  119.7 4.4 copy-start.12
  126.6 296.0 %reduce-scatter.3.cloned.1.call-start = ((), (), s32[]{:S(2)}) async-start(), calls=%async_computation.3 | async-start | bytes 2162688 | tf_op jit(solution)/shard_map/reduce_scatter | solution.py:45
  199.9 0.9 copy-start.6
  203.4 0.9 copy-start.1
  203.4 1.0 copy-start.8
  203.4 1.3 copy-start.9
  203.4 219.1 %copy-start.7 = (bf16[2,8,1024]{2,1,0:T(8,128)(2,1)S(1)}, bf16[2,8,1024]{2,1,0:T(8,128)(2,1)}, u32[]{:S(2)}) copy-start(bf16[2,8,1024]{2,1,0:T(8,128)(2,1)} %param.12) | copy-start | bytes 98308
  203.4 306.2 %all-gather.5.cloned.1.call-start = ((), (), s32[]{:S(2)}) async-start(), calls=%async_computation.4 | async-start | bytes 1081344 | tf_op jit(solution)/shard_map/all_gather | solution.py:53
  435.0 144.0 %all-reduce.5.cloned.1.call-start = ((), (), s32[]{:S(2)}) async-start(), calls=%async_computation.5 | async-start | bytes 3670016 | tf_op jit(solution)/shard_map/psum | solution.py:60
  513.4 292.0 %reduce-scatter.5.cloned.1.call-start = ((), (), s32[]{:S(2)}) async-start(), calls=%async_computation.6 | async-start | bytes 2162688 | tf_op jit(solution)/shard_map/reduce_scatter | solution.py:74
  579.0 3.6 copy-start.11
  582.6 1.3 copy-start.4
  582.6 1.8 copy-start.13
  587.1 0.7 copy-start.10
  665.3 4.1 copy-start.3
  665.3 4.0 copy-start.5
Sparse Core Ops, SparseCore 0:
  10.6 101.1 all-gather.2
  126.7 70.5 all-reduce.6
  203.6 218.9 reduce-scatter.2
  435.1 74.5 all-gather.4
  513.6 65.3 all-reduce.4
  587.2 218.2 reduce-scatter.4
where the time goes:
time: 816 us; the launch traced here: 815 us
  waiting for transfers between devices  663 us (81%)
  blocking collectives  85.8 us (11%)
  matrix products  26.8 us (3%)
  between operations  14.3 us (2%)
  local copies, waits for them, and re-layouts  12.6 us (2%)
  other arithmetic  12.2 us (1%)
    reduce_scatter x1, waiting for transfers between devices, on_device(): lax.psum_scatter(jnp.dot(act, down_weight, preferred_element_type=jnp.flo...  218 us
    reduce_scatter x1, waiting for transfers between devices, on_device(): lax.psum_scatter(first + second, 'wide', scatter_dimension=0, tiled=True)  131 us
    all_gather x1, waiting for transfers between devices, on_device(): whole_slab = lax.all_gather(hidden, 'wide', axis=1, tiled=True)  103 us
    psum x1, blocking collectives, on_device(): router_grad = lax.psum(router_part, 'wide')  75.8 us
    all_gather x1, waiting for transfers between devices, on_device(): out_all = lax.all_gather(out_grad, 'wide', axis=0, tiled=True)  74.6 us
    psum x1, waiting for transfers between devices, on_device(): gate, up = lax.psum((gate_part, up_part), 'narrow')  70.7 us
    psum x1, waiting for transfers between devices, on_device(): act_grad = lax.psum(act_part, 'narrow')  65.5 us
  transfers between devices with their start and end apart: 6, of which 6 were waited for; matrix products, arithmetic and copies ran while one was open for 2% of the time, Pallas kernels for 0%

commit v1 on v0

v1 whole, which is shorter than its diff:
```python
import functools

import jax
import jax.numpy as jnp
from jax import lax
from jax.experimental import pallas as pl
from jax.experimental.pallas import tpu as pltpu
from jax.sharding import PartitionSpec as P

MESH = pl.DeviceIdType.MESH
F32 = jnp.float32
BF16 = jnp.bfloat16

NX, NZ, NY = 4, 8, 4
TOK = 128
OWN = 16
ROWS = OWN * NX * NZ
SLOT = OWN * NX
CH = 2 * SLOT
NCH = ROWS // CH
EXT = 128
OFFSETS = (0, 1, -1, 2, -2, 3, -3, 4)


def encode(value, rows):
    wide = jnp.broadcast_to(value, (rows, EXT))
    high = wide.astype(BF16).astype(F32)
    lane = lax.broadcasted_iota(jnp.int32, (rows, EXT), 1)
    return jnp.where(lane < EXT // 2, high, wide - high).astype(BF16)


def decode(block):
    return block[:, 0:1].astype(F32) + block[:, EXT // 2 : EXT // 2 + 1].astype(F32)


def nt(a, b):
    return lax.dot_general(a, b, (((1,), (1,)), ((), ())), preferred_element_type=F32)


def tn(a, b):
    return lax.dot_general(a, b, (((0,), (0,)), ((), ())), preferred_element_type=F32)


def tiles(extent, step):
    return [(at, min(step, extent - at)) for at in range(0, extent, step)]


def kernel(
    D,
    F,
    hidden_hbm,
    rw_ref,
    teacher_ref,
    pos_ref,
    cot_ref,
    gw_hbm,
    uw_hbm,
    dw_hbm,
    hg_hbm,
    rg_ref,
    gg_hbm,
    ug_hbm,
    dg_hbm,
    hid,
    wgu,
    wd,
    agb,
    part,
    csend,
    crecv,
    ysend,
    yfirst,
    ysecond,
    ysum,
    gact,
    rgf,
    xsend,
    xrecv,
    zown,
    zsend,
    zrecv,
    lsend,
    lrecv,
    rparts_x,
    rparts_z,
    hg_out,
    gg_out,
    ug_out,
    dg_out,
    send_sem,
    recv_sem,
    local_sem,
):
    C = 3 * F + EXT
    H = C // 2
    wide, narrow = lax.axis_index("wide"), lax.axis_index("narrow")
    x, z = lax.div(wide, NZ), lax.rem(wide, NZ)
    y, core = lax.div(narrow, 2), lax.rem(narrow, 2)

    def at_x(d):
        return (lax.rem(x + d + NX, NX) * NZ + z, narrow)

    def at_z(d):
        return (x * NZ + lax.rem(z + d + NZ, NZ), narrow)

    def at_y(d):
        return (wide, lax.rem(y + d + NY, NY) * 2 + core)

    def at_n(d):
        return (wide, lax.rem(narrow + d, 2 * NY))

    sibling = (wide, y * 2 + (1 - core))

    count = [0]
    started = []

    def send(src, dst, device):
        i = count[0]
        count[0] += 1
        copy = pltpu.make_async_remote_copy(
            src_ref=src,
            dst_ref=dst,
            send_sem=send_sem.at[i],
            recv_sem=recv_sem.at[i],
            device_id=device,
            device_id_type=MESH,
        )
        copy.start()
        started.append(copy)
        return copy

    lcount = [0]

    def local(src, dst):
        copy = pltpu.make_async_copy(src, dst, local_sem.at[lcount[0]])
        lcount[0] += 1
        copy.start()
        return copy

    load_hid = local(hidden_hbm, hid)
    load_w = [
        local(gw_hbm, wgu.at[:, pl.ds(0, F)]),
        local(uw_hbm, wgu.at[:, pl.ds(F, F)]),
        local(dw_hbm, wd),
    ]

    barrier = pltpu.get_barrier_semaphore()
    peers = (
        [at_x(d) for d in range(1, NX)]
        + [at_z(d) for d in range(1, NZ)]
        + [at_n(d) for d in range(1, 2 * NY)]
    )
    for peer in peers:
        pl.semaphore_signal(barrier, inc=1, device_id=peer, device_id_type=MESH)

    sub = lax.broadcasted_iota(jnp.int32, (OWN, TOK), 0)
    lane = lax.broadcasted_iota(jnp.int32, (OWN, TOK), 1)
    sub_t = lax.broadcasted_iota(jnp.int32, (TOK, OWN), 0)
    lane_t = lax.broadcasted_iota(jnp.int32, (TOK, OWN), 1)
    pick = jnp.zeros((OWN, TOK), F32)
    place = jnp.zeros((TOK, OWN), F32)
    half_own, half_tok = OWN // 2, TOK // 2
    for r in range(OWN):
        s, j = r // half_own, r % half_own
        token = pos_ref[s, wide * half_own + j] - wide * half_tok + s * half_tok
        pick = jnp.where((sub == r) & (lane == token), 1.0, pick)
        place = jnp.where((lane_t == r) & (sub_t == token), 1.0, place)
    load_hid.wait()
    own_rows = jnp.dot(pick.astype(BF16), hid[...], preferred_element_type=F32)
    agb[0, pl.ds(0, OWN), :] = own_rows.astype(BF16)
    agb[1, pl.ds(0, OWN), :] = jnp.concatenate(
        [cot_ref[0].astype(F32), cot_ref[1].astype(F32)], axis=0
    ).astype(BF16)
    pl.semaphore_wait(barrier, len(peers))

    gx = [
        send(
            agb.at[:, pl.ds(0, OWN)],
            agb.at[:, pl.ds((NX - d) * OWN, OWN)],
            at_x(d),
        )
        for d in (1, 3, 2)
    ]

    eye = lax.broadcasted_iota(jnp.int32, (TOK, TOK), 0) == lax.broadcasted_iota(
        jnp.int32, (TOK, TOK), 1
    )
    logit_col = jnp.sum(hid[...].astype(F32) * rw_ref[...], axis=1, keepdims=True)
    logit_row = jnp.sum(jnp.where(eye, logit_col, 0.0), axis=0, keepdims=True)
    lsend[...] = jnp.broadcast_to(logit_row, (8, TOK))
    lg = [send(lsend, lrecv.at[d - 1], at_n(d)) for d in range(1, 2 * NY)]

    for copy in gx:
        copy.wait_recv()

    def slot(k, n=1):
        return pl.ds(k * SLOT, n * SLOT)

    def gather_z(src, dst, d, which=None):
        if which is None:
            return send(agb.at[:, slot(src)], agb.at[:, slot(dst)], at_z(d))
        return send(agb.at[which, slot(src)], agb.at[which, slot(dst)], at_z(d))

    gz = {0: [gather_z(0, 1, -1), gather_z(0, 2, 1)]}
    for copy in load_w:
        copy.wait()

    core_out, y_first, y_second, g_first, g_second, core_back, x_out, z_out = (
        {} for _ in range(8)
    )

    def block(j, base=0):
        return pl.ds(pl.multiple_of(base + lax.rem(y + j + NY, NY) * OWN, OWN), OWN)

    def stage1(i):
        for copy in gz[i]:
            copy.wait_recv()
        if i == 0:
            gz[1] = [gather_z(1, 3, -1), gather_z(2, 4, 1)]
        elif i == 1:
            gz[2] = [gather_z(3, 5, -1), gather_z(4, 6, 1)]
        elif i == 2:
            gz[3] = [gather_z(5, 7, -1, 0), gather_z(6, 7, 1, 1)]
        rows = pl.ds(i * CH, CH)

        @pl.loop(0, 2 * F // 256)
        def _(t):
            cols = pl.ds(pl.multiple_of(t * 256, 256), 256)
            part[i, :, cols] = jnp.dot(
                agb[0, rows, :], wgu[:, cols], preferred_element_type=F32
            )

        for at, n in tiles(F, 256):
            part[i, :, pl.ds(2 * F + at, n)] = nt(agb[1, rows, :], wd[pl.ds(at, n), :])
        logit = jnp.sum(agb[0, rows, :].astype(F32) * rw_ref[...], axis=1, keepdims=True)
        part[i, :, pl.ds(3 * F, EXT)] = jnp.broadcast_to(logit, (CH, EXT))
        other = pl.ds(pl.multiple_of((1 - core) * SLOT, SLOT), SLOT)
        csend[i, :, pl.ds(0, 3 * F)] = part[i, other, pl.ds(0, 3 * F)].astype(BF16)
        csend[i, :, pl.ds(3 * F, EXT)] = encode(
            part[i, other, pl.ds(3 * F, EXT)][:, 0:1], SLOT
        )
        core_out[i] = send(csend.at[i], crecv.at[i], sibling)

    def stage2(i):
        core_out[i].wait_recv()
        base = pl.multiple_of(core * SLOT, SLOT)
        mine = pl.ds(base, SLOT)
        total = part[i, mine, pl.ds(0, 3 * F)] + crecv[i, :, pl.ds(0, 3 * F)].astype(F32)
        part[i, mine, pl.ds(0, 3 * F)] = total
        ysend[i, :, pl.ds(0, 3 * F)] = total.astype(BF16)
        logit = part[i, mine, pl.ds(3 * F, EXT)][:, 0:1] + decode(
            crecv[i, :, pl.ds(3 * F, EXT)]
        )
        part[i, mine, pl.ds(3 * F, EXT)] = jnp.broadcast_to(logit, (SLOT, EXT))
        ysend[i, :, pl.ds(3 * F, EXT)] = encode(logit, SLOT)
        left, right = pl.ds(0, H), pl.ds(H, H)
        y_first[i] = [
            send(ysend.at[i, block(2), left], yfirst.at[i, 0], at_y(1)),
            send(ysend.at[i, block(2), right], yfirst.at[i, 1], at_y(-1)),
            send(ysend.at[i, block(1), right], ysecond.at[i, 0, :, right], at_y(1)),
            send(ysend.at[i, block(-1), left], ysecond.at[i, 1, :, left], at_y(-1)),
        ]

    def stage3(i):
        y_first[i][0].wait_recv()
        y_first[i][1].wait_recv()
        base = core * SLOT
        left, right = pl.ds(0, H), pl.ds(H, H)
        ysum[i, 0] = (
            part[i, block(1, base), left] + yfirst[i, 0].astype(F32)
        ).astype(BF16)
        a = send(ysum.at[i, 0], ysecond.at[i, 0, :, left], at_y(1))
        ysum[i, 1, :, pl.ds(0, H - EXT)] = (
            part[i, block(-1, base), pl.ds(H, H - EXT)]
            + yfirst[i, 1, :, pl.ds(0, H - EXT)].astype(F32)
        ).astype(BF16)
        logit = part[i, block(-1, base), pl.ds(3 * F, EXT)][:, 0:1] + decode(
            yfirst[i, 1, :, pl.ds(H - EXT, EXT)]
        )
        ysum[i, 1, :, pl.ds(H - EXT, EXT)] = encode(logit, OWN)
        b = send(ysum.at[i, 1], ysecond.at[i, 1, :, right], at_y(-1))
        y_second[i] = [a, b]

    def stage4(i):
        for copy in y_first[i][2:] + y_second[i]:
            copy.wait_recv()
        own = block(0, core * SLOT)

        def total(at):
            cols = pl.ds(at, F)
            return (
                part[i, own, cols]
                + ysecond[i, 0, :, cols].astype(F32)
                + ysecond[i, 1, :, cols].astype(F32)
            )

        ext = pl.ds(3 * F, EXT)
        logit = (
            part[i, own, ext][:, 0:1]
            + decode(ysecond[i, 0, :, ext])
            + decode(ysecond[i, 1, :, ext])
        )
        scale = jax.nn.sigmoid(logit)
        gate, up, raw = total(0), total(F), total(2 * F)
        sig = jax.nn.sigmoid(gate)
        silu = gate * sig
        act = silu * up
        act_grad = scale * raw
        out = block(0, i * CH + core * SLOT)
        gact[out, pl.ds(0, F)] = (act_grad * up * sig * (1.0 + gate * (1.0 - sig))).astype(BF16)
        gact[out, pl.ds(F, F)] = (act_grad * silu).astype(BF16)
        gact[out, pl.ds(2 * F, F)] = (scale * act).astype(BF16)
        dots = jnp.sum(act * raw, axis=1, keepdims=True)
        gact[out, ext] = encode(scale * (1.0 - scale) * dots, OWN)
        g_first[i] = [
            send(gact.at[out], gact.at[out], at_y(1)),
            send(gact.at[out], gact.at[out], at_y(-1)),
        ]

    def stage5(i):
        base = i * CH + core * SLOT
        g_first[i][0].wait_recv()
        left = gact.at[block(-1, base), pl.ds(0, H)]
        a = send(left, left, at_y(1))
        g_first[i][1].wait_recv()
        right = gact.at[block(1, base), pl.ds(H, H)]
        b = send(right, right, at_y(-1))
        g_second[i] = [a, b]

    def stage6(i):
        for copy in g_second[i]:
            copy.wait_recv()
        half = gact.at[pl.ds(pl.multiple_of(i * CH + core * SLOT, SLOT), SLOT)]
        core_back[i] = send(half, half, sibling)

    def stage7(i):
        core_back[i].wait_recv()
        rows = pl.ds(i * CH, CH)

        @pl.loop(0, D // 256)
        def _(t):
            cols = pl.ds(pl.multiple_of(t * 256, 256), 256)
            out = nt(gact[rows, pl.ds(0, 2 * F)], wgu[cols, :])
            for s in range(2):
                for j in range(NX):
                    piece = out[s * SLOT + j * OWN : s * SLOT + (j + 1) * OWN]
                    if j == 0:
                        rgf[i, s, :, cols] = piece
                    else:
                        xsend[i, s, j - 1, :, cols] = piece.astype(BF16)

        for s in range(2):
            for j in range(NX):
                ext = gact[pl.ds(i * CH + s * SLOT + j * OWN, OWN), pl.ds(3 * F, EXT)]
                if j == 0:
                    rgf[i, s, :, pl.ds(D, EXT)] = jnp.broadcast_to(decode(ext), (OWN, EXT))
                else:
                    xsend[i, s, j - 1, :, pl.ds(D, EXT)] = ext
        x_out[i] = [
            send(xsend.at[i, :, j - 1], xrecv.at[i, j - 1], at_x(j)) for j in (2, 1, 3)
        ]

    def stage8(i):
        for copy in x_out[i]:
            copy.wait_recv()
        for s in range(2):
            k = 2 * i + s
            total = rgf[i, s, :, pl.ds(0, D)]
            extra = rgf[i, s, :, pl.ds(D, EXT)][:, 0:1]
            for j in range(NX - 1):
                total = total + xrecv[i, j, s, :, pl.ds(0, D)].astype(F32)
                extra = extra + decode(xrecv[i, j, s, :, pl.ds(D, EXT)])
            if k == 0:
                zown[:, pl.ds(0, D)] = total
                zown[:, pl.ds(D, EXT)] = jnp.broadcast_to(extra, (OWN, EXT))
            else:
                zsend[k - 1, :, pl.ds(0, D)] = total.astype(BF16)
                zsend[k - 1, :, pl.ds(D, EXT)] = encode(extra, OWN)
                z_out[k] = send(zsend.at[k - 1], zrecv.at[k - 1], at_z(OFFSETS[k]))

    for i in range(NCH):
        stage1(i)
        if i >= 1:
            stage5(i - 1)
        stage2(i)
        if i >= 1:
            stage6(i - 1)
        if i >= 2:
            stage8(i - 2)
        stage3(i)
        if i >= 1:
            stage7(i - 1)
        stage4(i)
    stage5(NCH - 1)

    for copy in lg:
        copy.wait_recv()
    logits = lsend[0:1, :]
    for d in range(2 * NY - 1):
        logits = logits + lrecv[d, 0:1, :]
    logit_col = jnp.sum(jnp.where(eye, logits, 0.0), axis=1, keepdims=True)
    eye_half = lax.broadcasted_iota(jnp.int32, (half_tok, half_tok), 0) == (
        lax.broadcasted_iota(jnp.int32, (half_tok, half_tok), 1)
    )
    teacher = jnp.concatenate(
        [
            jnp.sum(jnp.where(eye_half, teacher_ref[s : s + 1, :], 0.0), axis=1, keepdims=True)
            for s in range(2)
        ],
        axis=0,
    )
    token_grad = jax.nn.sigmoid(logit_col) - teacher
    router = jnp.sum(token_grad * hid[...].astype(F32), axis=0, keepdims=True)

    stage6(NCH - 1)
    stage8(NCH - 2)
    stage7(NCH - 1)

    routed = tn(gact[:, pl.ds(3 * F, EXT)], agb[0])
    router = router + routed[0:1] + routed[EXT // 2 : EXT // 2 + 1]
    for a in range(D // 128):
        rparts_x[x, a : a + 1, :] = router[:, a * 128 : (a + 1) * 128]
    rx = [send(rparts_x.at[x], rparts_x.at[x], at_x(d)) for d in range(1, NX)]

    @pl.loop(0, D // 256)
    def _(t):
        cols = pl.ds(pl.multiple_of(t * 256, 256), 256)
        out = tn(agb[0, :, cols], gact[:, pl.ds(0, 2 * F)])
        gg_out[cols, :] = out[:, :F].astype(BF16)
        ug_out[cols, :] = out[:, F:].astype(BF16)

    stores = [local(gg_out, gg_hbm), local(ug_out, ug_hbm)]
    stage8(NCH - 1)

    for copy in rx:
        copy.wait_recv()
    rparts_z[z] = rparts_x[0] + rparts_x[1] + rparts_x[2] + rparts_x[3]
    rz = [send(rparts_z.at[z], rparts_z.at[z], at_z(d)) for d in range(1, NZ)]

    @pl.loop(0, F // 128)
    def _(t):
        cols = pl.ds(pl.multiple_of(t * 128, 128), 128)
        acts = gact[:, pl.ds(pl.multiple_of(2 * F + t * 128, 128), 128)]
        dg_out[cols, :] = tn(acts, agb[1]).astype(BF16)

    stores.append(local(dg_out, dg_hbm))

    for k in range(1, NZ):
        z_out[k].wait_recv()
    total = zown[:, pl.ds(0, D)]
    extra = zown[:, pl.ds(D, EXT)][:, 0:1]
    for k in range(NZ - 1):
        total = total + zrecv[k, :, pl.ds(0, D)].astype(F32)
        extra = extra + decode(zrecv[k, :, pl.ds(D, EXT)])
    total = total + extra * rw_ref[...]
    high = total.astype(BF16)
    low = (total - high.astype(F32)).astype(BF16)
    place16 = place.astype(BF16)
    hg_out[...] = (
        token_grad * rw_ref[...]
        + jnp.dot(place16, high, preferred_element_type=F32)
        + jnp.dot(place16, low, preferred_element_type=F32)
    ).astype(BF16)
    stores.append(local(hg_out, hg_hbm))

    for copy in rz:
        copy.wait_recv()
    final = rparts_z[0]
    for k in range(1, NZ):
        final = final + rparts_z[k]
    for a in range(D // 128):
        rg_ref[:, a * 128 : (a + 1) * 128] = final[a : a + 1, :]

    for copy in started:
        copy.wait_send()
    for copy in stores:
        copy.wait()


def on_device(
    hidden, router_weight, teacher, positions, cotangent, gate_weight, up_weight, down_weight
):
    slabs, rows_dev, D = hidden.shape
    F = gate_weight.shape[1]
    C = 3 * F + EXT
    vmem = pl.BlockSpec(memory_space=pltpu.VMEM)
    smem = pl.BlockSpec(memory_space=pltpu.SMEM)
    hbm = pl.BlockSpec(memory_space=pl.ANY)
    copies = 3 + 8 + 7 + NCH * 15 + 7 + 3 + 7
    hidden_grad, router_grad, gate_grad, up_grad, down_grad = pl.pallas_call(
        functools.partial(kernel, D, F),
        out_shape=(
            jax.ShapeDtypeStruct((TOK, D), BF16),
            jax.ShapeDtypeStruct((1, D), F32),
            jax.ShapeDtypeStruct((D, F), BF16),
            jax.ShapeDtypeStruct((D, F), BF16),
            jax.ShapeDtypeStruct((F, D), BF16),
        ),
        in_specs=[hbm, vmem, vmem, smem, vmem, hbm, hbm, hbm],
        out_specs=(hbm, vmem, hbm, hbm, hbm),
        scratch_shapes=[
            pltpu.VMEM((TOK, D), BF16),
            pltpu.VMEM((D, 2 * F), BF16),
            pltpu.VMEM((F, D), BF16),
            pltpu.VMEM((2, ROWS, D), BF16),
            pltpu.VMEM((NCH, CH, C), F32),
            pltpu.VMEM((NCH, SLOT, C), BF16),
            pltpu.VMEM((NCH, SLOT, C), BF16),
            pltpu.VMEM((NCH, SLOT, C), BF16),
            pltpu.VMEM((NCH, 2, OWN, C // 2), BF16),
            pltpu.VMEM((NCH, 2, OWN, C), BF16),
            pltpu.VMEM((NCH, 2, OWN, C // 2), BF16),
            pltpu.VMEM((ROWS, C), BF16),
            pltpu.VMEM((NCH, 2, OWN, D + EXT), F32),
            pltpu.VMEM((NCH, 2, NX - 1, OWN, D + EXT), BF16),
            pltpu.VMEM((NCH, NX - 1, 2, OWN, D + EXT), BF16),
            pltpu.VMEM((OWN, D + EXT), F32),
            pltpu.VMEM((NZ - 1, OWN, D + EXT), BF16),
            pltpu.VMEM((NZ - 1, OWN, D + EXT), BF16),
            pltpu.VMEM((8, TOK), F32),
            pltpu.VMEM((2 * NY - 1, 8, TOK), F32),
            pltpu.VMEM((NX, D // 128, 128), F32),
            pltpu.VMEM((NZ, D // 128, 128), F32),
            pltpu.VMEM((TOK, D), BF16),
            pltpu.VMEM((D, F), BF16),
            pltpu.VMEM((D, F), BF16),
            pltpu.VMEM((F, D), BF16),
            pltpu.SemaphoreType.DMA((copies,)),
            pltpu.SemaphoreType.DMA((copies,)),
            pltpu.SemaphoreType.DMA((8,)),
        ],
        compiler_params=pltpu.CompilerParams(
            collective_id=0,
            has_side_effects=True,
            vmem_limit_bytes=58 * 1024 * 1024,
        ),
    )(
        hidden.reshape(slabs * rows_dev, D),
        router_weight.reshape(1, D),
        teacher,
        positions,
        cotangent,
        gate_weight,
        up_weight,
        down_weight,
    )
    return (
        hidden_grad.reshape(hidden.shape),
        router_grad.reshape(D),
        gate_grad,
        up_grad,
        down_grad,
    )


def solution(mesh):
    in_specs = (
        P(None, "wide", "narrow"),
        P("narrow"),
        P(None, "wide"),
        P(),
        P(None, "wide", "narrow"),
        P("narrow", "wide"),
        P("narrow", "wide"),
        P("wide", "narrow"),
    )
    out_specs = (
        P(None, "wide", "narrow"),
        P("narrow"),
        P("narrow", "wide"),
        P("narrow", "wide"),
        P("wide", "narrow"),
    )
    return jax.shard_map(
        on_device, mesh=mesh, in_specs=in_specs, out_specs=out_specs, check_vma=False
    )
```

time: 816 us -> 106 us (0.13)
  the two profiles are of different devices: /device:TPU:8 before, /device:TPU:32 now
where the time goes in v1:
time: 106 us
  Pallas kernels  96.3 us (91%)
  local copies, waits for them, and re-layouts  9.34 us (9%)
    pallas_call x1, Pallas kernels, on_device(): pl.pallas_call(functools.partial(kernel, D, F), out_shape=(jax.ShapeDtype...  96.3 us
    unnamed x9, local copies, waits for them, and re-layouts  9.34 us

profile of v1, /device:TPU:32, one launch (start us, length us, event | category | flops | bytes accessed | tf_op | source)
XLA Modules:
  0.0 106.2 jit_solution(17232155248079772767)
XLA Ops:
  0.6 96.3 %shard_map.119 = (bf16[128,1024]{1,0:T(8,128)(2,1)}, f32[1,1024]{1,0:T(1,128)}, bf16[1024,896]{1,0:T(8,128)(2,1)}, bf16[1024,896]{1,0:T(8,128)(2,1)}, bf16[896,1024]{1,0:T(8,128)(2,1)}) custom-call(bf16[128,1024]{1,0:T(8,128)(2,1)} %bitcast.4, f32[1,1024]{1,0:T(1,128)} %bitcast.6, f32[2,64]{1,0:T(2,128)} %teacher_ref.1, s32[2,256]{1,0:T(2,128)} %pos_ref.1, ...), custom_call_target="tpu_custom_call" | custom-call | tf_op jit(solution)/shard_map/pallas_call | solution.py:490
  96.9 1.7 %copy.18 = bf16[2,64,1024]{2,1,0:T(8,128)(2,1)} copy(bf16[2,64,1024]{2,1,0:T(8,128)(2,1)} %bitcast.5) | data formatting | bytes 524288
  98.6 1.3 %copy.19 = f32[1024]{0:T(1024)} copy(f32[1024]{0:T(1024)} %bitcast.7) | data formatting | bytes 8192
  99.8 0.0 copy-start.1
  99.8 3.0 %copy.20 = bf16[1024,896]{1,0:T(8,128)(2,1)} copy(bf16[1024,896]{1,0:T(8,128)(2,1)} %get-tuple-element.22) | data formatting | bytes 3670016
  102.8 0.0 copy-done.1
  102.8 0.0 copy-start
  102.9 1.2 %copy.21 = bf16[1024,896]{1,0:T(8,128)(2,1)} copy(bf16[1024,896]{1,0:T(8,128)(2,1)S(1)} %copy-done.1) | data formatting | bytes 3670016
  104.1 0.9 copy-done
  105.0 1.2 %copy.22 = bf16[896,1024]{1,0:T(8,128)(2,1)} copy(bf16[896,1024]{1,0:T(8,128)(2,1)S(1)} %copy-done) | data formatting | bytes 3670016
Async XLA Ops:
  99.8 3.0 %copy-start.1 = (bf16[1024,896]{1,0:T(8,128)(2,1)S(1)}, bf16[1024,896]{1,0:T(8,128)(2,1)}, u32[]{:S(2)}) copy-start(bf16[1024,896]{1,0:T(8,128)(2,1)} %get-tuple-element.23) | copy-start | bytes 5505028
  102.8 2.2 %copy-start = (bf16[896,1024]{1,0:T(8,128)(2,1)S(1)}, bf16[896,1024]{1,0:T(8,128)(2,1)}, u32[]{:S(2)}) copy-start(bf16[896,1024]{1,0:T(8,128)(2,1)} %get-tuple-element.24) | copy-start | bytes 5505028

commit v2 on v1

--- a/solution.py
+++ b/solution.py
@@ -20,6 +20,15 @@
 NCH = ROWS // CH
 EXT = 128
 OFFSETS = (0, 1, -1, 2, -2, 3, -3, 4)
+
+ORDER = (
+    "GR:0", "GC:0", "T:0", "GR:1", "GC:1", "A:0", "GR:2", "B:0",
+    "GC:2", "A:1", "GR:3", "D:0", "B:1", "GC:3", "A:2", "B:2",
+    "A:3", "E:0", "D:1", "B:3", "F:0", "G:0", "D:2", "E:1",
+    "D:3", "H:0", "F:1", "E:2", "G:1", "E:3", "F:2", "G:2",
+    "F:3", "G:3", "H:1", "RX:0", "WI:0", "WI:1", "WI:2", "RZ:0",
+    "WI:3", "H:2", "WO:0", "WO:1", "WO:2", "WO:3", "H:3",
+)
 
 
 def encode(value, rows):
@@ -56,11 +65,11 @@
     gw_hbm,
     uw_hbm,
     dw_hbm,
-    hg_hbm,
+    hg_out,
     rg_ref,
-    gg_hbm,
-    ug_hbm,
-    dg_hbm,
+    gg_out,
+    ug_out,
+    dg_out,
     hid,
     wgu,
     wd,
@@ -69,9 +78,7 @@
     csend,
     crecv,
     ysend,
-    yfirst,
-    ysecond,
-    ysum,
+    yrecv,
     gact,
     rgf,
     xsend,
@@ -83,10 +90,7 @@
     lrecv,
     rparts_x,
     rparts_z,
-    hg_out,
-    gg_out,
-    ug_out,
-    dg_out,
+    tgrad,
     send_sem,
     recv_sem,
     local_sem,
@@ -173,14 +177,13 @@
     ).astype(BF16)
     pl.semaphore_wait(barrier, len(peers))
 
-    gx = [
-        send(
-            agb.at[:, pl.ds(0, OWN)],
-            agb.at[:, pl.ds((NX - d) * OWN, OWN)],
-            at_x(d),
-        )
-        for d in (1, 3, 2)
-    ]
+    def gather_x(which):
+        own = agb.at[which, pl.ds(0, OWN)]
+        return [
+            send(own, agb.at[which, pl.ds((NX - d) * OWN, OWN)], at_x(d)) for d in (2, 1, 3)
+        ]
+
+    gx = {0: gather_x(0)}
 
     eye = lax.broadcasted_iota(jnp.int32, (TOK, TOK), 0) == lax.broadcasted_iota(
         jnp.int32, (TOK, TOK), 1
@@ -190,42 +193,50 @@
     lsend[...] = jnp.broadcast_to(logit_row, (8, TOK))
     lg = [send(lsend, lrecv.at[d - 1], at_n(d)) for d in range(1, 2 * NY)]
 
-    for copy in gx:
-        copy.wait_recv()
-
-    def slot(k, n=1):
-        return pl.ds(k * SLOT, n * SLOT)
-
-    def gather_z(src, dst, d, which=None):
-        if which is None:
-            return send(agb.at[:, slot(src)], agb.at[:, slot(dst)], at_z(d))
-        return send(agb.at[which, slot(src)], agb.at[which, slot(dst)], at_z(d))
-
-    gz = {0: [gather_z(0, 1, -1), gather_z(0, 2, 1)]}
-    for copy in load_w:
-        copy.wait()
-
-    core_out, y_first, y_second, g_first, g_second, core_back, x_out, z_out = (
-        {} for _ in range(8)
-    )
+    gz = {}
+
+    def ring(which, src, dst, d, at=0, n=SLOT):
+        return send(
+            agb.at[which, pl.ds(src * SLOT + at, n)],
+            agb.at[which, pl.ds(dst * SLOT + at, n)],
+            at_z(d),
+        )
+
+    def gather(which, step):
+        for copy in gx[which] if step == 0 else gz[which, step]:
+            copy.wait_recv()
+        if step == 0:
+            gz[which, 1] = [ring(which, 0, 1, -1), ring(which, 0, 2, 1)]
+            if which == 0:
+                gx[1] = gather_x(1)
+        elif step == 1:
+            gz[which, 2] = [ring(which, 1, 3, -1), ring(which, 2, 4, 1)]
+        elif step == 2:
+            gz[which, 3] = [ring(which, 3, 5, -1), ring(which, 4, 6, 1)]
+        elif step == 3:
+            half = SLOT // 2
+            gz[which, 4] = [
+                ring(which, 5, 7, -1, 0, half),
+                ring(which, 6, 7, 1, half, half),
+            ]
+
+    core_out, y_out, g_first, g_second, core_back, x_out, z_out = ({} for _ in range(7))
 
     def block(j, base=0):
         return pl.ds(pl.multiple_of(base + lax.rem(y + j + NY, NY) * OWN, OWN), OWN)
 
     def stage1(i):
-        for copy in gz[i]:
-            copy.wait_recv()
+        rows = pl.ds(i * CH, CH)
         if i == 0:
-            gz[1] = [gather_z(1, 3, -1), gather_z(2, 4, 1)]
-        elif i == 1:
-            gz[2] = [gather_z(3, 5, -1), gather_z(4, 6, 1)]
-        elif i == 2:
-            gz[3] = [gather_z(5, 7, -1, 0), gather_z(6, 7, 1, 1)]
-        rows = pl.ds(i * CH, CH)
-
-        @pl.loop(0, 2 * F // 256)
-        def _(t):
-            cols = pl.ds(pl.multiple_of(t * 256, 256), 256)
+            for copy in load_w:
+                copy.wait()
+        if i == NCH - 1:
+            for which in (0, 1):
+                for copy in gz[which, 4]:
+                    copy.wait_recv()
+
+        for at, n in tiles(2 * F, 256):
+            cols = pl.ds(at, n)
             part[i, :, cols] = jnp.dot(
                 agb[0, rows, :], wgu[:, cols], preferred_element_type=F32
             )
@@ -253,53 +264,26 @@
         )
         part[i, mine, pl.ds(3 * F, EXT)] = jnp.broadcast_to(logit, (SLOT, EXT))
         ysend[i, :, pl.ds(3 * F, EXT)] = encode(logit, SLOT)
-        left, right = pl.ds(0, H), pl.ds(H, H)
-        y_first[i] = [
-            send(ysend.at[i, block(2), left], yfirst.at[i, 0], at_y(1)),
-            send(ysend.at[i, block(2), right], yfirst.at[i, 1], at_y(-1)),
-            send(ysend.at[i, block(1), right], ysecond.at[i, 0, :, right], at_y(1)),
-            send(ysend.at[i, block(-1), left], ysecond.at[i, 1, :, left], at_y(-1)),
+        y_out[i] = [
+            send(ysend.at[i, block(d)], yrecv.at[i, d - 1], at_y(d)) for d in (2, 1, 3)
         ]
 
-    def stage3(i):
-        y_first[i][0].wait_recv()
-        y_first[i][1].wait_recv()
-        base = core * SLOT
-        left, right = pl.ds(0, H), pl.ds(H, H)
-        ysum[i, 0] = (
-            part[i, block(1, base), left] + yfirst[i, 0].astype(F32)
-        ).astype(BF16)
-        a = send(ysum.at[i, 0], ysecond.at[i, 0, :, left], at_y(1))
-        ysum[i, 1, :, pl.ds(0, H - EXT)] = (
-            part[i, block(-1, base), pl.ds(H, H - EXT)]
-            + yfirst[i, 1, :, pl.ds(0, H - EXT)].astype(F32)
-        ).astype(BF16)
-        logit = part[i, block(-1, base), pl.ds(3 * F, EXT)][:, 0:1] + decode(
-            yfirst[i, 1, :, pl.ds(H - EXT, EXT)]
-        )
-        ysum[i, 1, :, pl.ds(H - EXT, EXT)] = encode(logit, OWN)
-        b = send(ysum.at[i, 1], ysecond.at[i, 1, :, right], at_y(-1))
-        y_second[i] = [a, b]
-
     def stage4(i):
-        for copy in y_first[i][2:] + y_second[i]:
+        for copy in y_out[i]:
             copy.wait_recv()
         own = block(0, core * SLOT)
 
         def total(at):
             cols = pl.ds(at, F)
-            return (
-                part[i, own, cols]
-                + ysecond[i, 0, :, cols].astype(F32)
-                + ysecond[i, 1, :, cols].astype(F32)
-            )
+            value = part[i, own, cols]
+            for d in range(NY - 1):
+                value = value + yrecv[i, d, :, cols].astype(F32)
+            return value
 
         ext = pl.ds(3 * F, EXT)
-        logit = (
-            part[i, own, ext][:, 0:1]
-            + decode(ysecond[i, 0, :, ext])
-            + decode(ysecond[i, 1, :, ext])
-        )
+        logit = part[i, own, ext][:, 0:1]
+        for d in range(NY - 1):
+            logit = logit + decode(yrecv[i, d, :, ext])
         scale = jax.nn.sigmoid(logit)
         gate, up, raw = total(0), total(F), total(2 * F)
         sig = jax.nn.sigmoid(gate)
@@ -337,9 +321,8 @@
         core_back[i].wait_recv()
         rows = pl.ds(i * CH, CH)
 
-        @pl.loop(0, D // 256)
-        def _(t):
-            cols = pl.ds(pl.multiple_of(t * 256, 256), 256)
+        for at, n in tiles(D, 256):
+            cols = pl.ds(at, n)
             out = nt(gact[rows, pl.ds(0, 2 * F)], wgu[cols, :])
             for s in range(2):
                 for j in range(NX):
@@ -378,72 +361,73 @@
                 zsend[k - 1, :, pl.ds(D, EXT)] = encode(extra, OWN)
                 z_out[k] = send(zsend.at[k - 1], zrecv.at[k - 1], at_z(OFFSETS[k]))
 
-    for i in range(NCH):
-        stage1(i)
-        if i >= 1:
-            stage5(i - 1)
-        stage2(i)
-        if i >= 1:
-            stage6(i - 1)
-        if i >= 2:
-            stage8(i - 2)
-        stage3(i)
-        if i >= 1:
-            stage7(i - 1)
-        stage4(i)
-    stage5(NCH - 1)
-
-    for copy in lg:
-        copy.wait_recv()
-    logits = lsend[0:1, :]
-    for d in range(2 * NY - 1):
-        logits = logits + lrecv[d, 0:1, :]
-    logit_col = jnp.sum(jnp.where(eye, logits, 0.0), axis=1, keepdims=True)
-    eye_half = lax.broadcasted_iota(jnp.int32, (half_tok, half_tok), 0) == (
-        lax.broadcasted_iota(jnp.int32, (half_tok, half_tok), 1)
-    )
-    teacher = jnp.concatenate(
-        [
-            jnp.sum(jnp.where(eye_half, teacher_ref[s : s + 1, :], 0.0), axis=1, keepdims=True)
-            for s in range(2)
-        ],
-        axis=0,
-    )
-    token_grad = jax.nn.sigmoid(logit_col) - teacher
-    router = jnp.sum(token_grad * hid[...].astype(F32), axis=0, keepdims=True)
-
-    stage6(NCH - 1)
-    stage8(NCH - 2)
-    stage7(NCH - 1)
-
-    routed = tn(gact[:, pl.ds(3 * F, EXT)], agb[0])
-    router = router + routed[0:1] + routed[EXT // 2 : EXT // 2 + 1]
-    for a in range(D // 128):
-        rparts_x[x, a : a + 1, :] = router[:, a * 128 : (a + 1) * 128]
-    rx = [send(rparts_x.at[x], rparts_x.at[x], at_x(d)) for d in range(1, NX)]
-
-    @pl.loop(0, D // 256)
-    def _(t):
-        cols = pl.ds(pl.multiple_of(t * 256, 256), 256)
+    held = {}
+
+    def own_tokens():
+        for copy in lg:
+            copy.wait_recv()
+        logits = lsend[0:1, :]
+        for d in range(2 * NY - 1):
+            logits = logits + lrecv[d, 0:1, :]
+        logit_col = jnp.sum(jnp.where(eye, logits, 0.0), axis=1, keepdims=True)
+        eye_half = lax.broadcasted_iota(jnp.int32, (half_tok, half_tok), 0) == (
+            lax.broadcasted_iota(jnp.int32, (half_tok, half_tok), 1)
+        )
+        teacher = jnp.concatenate(
+            [
+                jnp.sum(jnp.where(eye_half, teacher_ref[s : s + 1, :], 0.0), axis=1, keepdims=True)
+                for s in range(2)
+            ],
+            axis=0,
+        )
+        grad = jax.nn.sigmoid(logit_col) - teacher
+        router = jnp.sum(grad * hid[...].astype(F32), axis=0, keepdims=True)
+        for a in range(D // 128):
+            rparts_x[x, a : a + 1, :] = router[:, a * 128 : (a + 1) * 128]
+        tgrad[...] = jnp.broadcast_to(grad, (TOK, 128))
+
+    def router_x():
+        routed = tn(gact[:, pl.ds(3 * F, EXT)], agb[0])
+        routed = routed[0:1] + routed[EXT // 2 : EXT // 2 + 1]
+        for a in range(D // 128):
+            rparts_x[x, a : a + 1, :] += routed[:, a * 128 : (a + 1) * 128]
+        held["rx"] = [send(rparts_x.at[x], rparts_x.at[x], at_x(d)) for d in range(1, NX)]
+
+    def router_z():
+        for copy in held["rx"]:
+            copy.wait_recv()
+        rparts_z[z] = rparts_x[0] + rparts_x[1] + rparts_x[2] + rparts_x[3]
+        held["rz"] = [send(rparts_z.at[z], rparts_z.at[z], at_z(d)) for d in range(1, NZ)]
+
+    def grads_in(t):
+        cols = pl.ds(t * 256, 256)
         out = tn(agb[0, :, cols], gact[:, pl.ds(0, 2 * F)])
         gg_out[cols, :] = out[:, :F].astype(BF16)
         ug_out[cols, :] = out[:, F:].astype(BF16)
 
-    stores = [local(gg_out, gg_hbm), local(ug_out, ug_hbm)]
-    stage8(NCH - 1)
-
-    for copy in rx:
-        copy.wait_recv()
-    rparts_z[z] = rparts_x[0] + rparts_x[1] + rparts_x[2] + rparts_x[3]
-    rz = [send(rparts_z.at[z], rparts_z.at[z], at_z(d)) for d in range(1, NZ)]
-
-    @pl.loop(0, F // 128)
-    def _(t):
-        cols = pl.ds(pl.multiple_of(t * 128, 128), 128)
-        acts = gact[:, pl.ds(pl.multiple_of(2 * F + t * 128, 128), 128)]
-        dg_out[cols, :] = tn(acts, agb[1]).astype(BF16)
-
-    stores.append(local(dg_out, dg_hbm))
+    def grads_out(t):
+        at, n = tiles(F, 256)[t]
+        dg_out[pl.ds(at, n), :] = tn(gact[:, pl.ds(2 * F + at, n)], agb[1]).astype(BF16)
+
+    tasks = {
+        "GR": lambda step: gather(0, step),
+        "GC": lambda step: gather(1, step),
+        "A": stage1,
+        "B": stage2,
+        "D": stage4,
+        "E": stage5,
+        "F": stage6,
+        "G": stage7,
+        "H": stage8,
+        "T": lambda _: own_tokens(),
+        "RX": lambda _: router_x(),
+        "RZ": lambda _: router_z(),
+        "WI": grads_in,
+        "WO": grads_out,
+    }
+    for task in ORDER:
+        name, step = task.split(":")
+        tasks[name](int(step))
 
     for k in range(1, NZ):
         z_out[k].wait_recv()
@@ -457,13 +441,12 @@
     low = (total - high.astype(F32)).astype(BF16)
     place16 = place.astype(BF16)
     hg_out[...] = (
-        token_grad * rw_ref[...]
+        tgrad[:, 0:1] * rw_ref[...]
         + jnp.dot(place16, high, preferred_element_type=F32)
         + jnp.dot(place16, low, preferred_element_type=F32)
     ).astype(BF16)
-    stores.append(local(hg_out, hg_hbm))
-
-    for copy in rz:
+
+    for copy in held["rz"]:
         copy.wait_recv()
     final = rparts_z[0]
     for k in range(1, NZ):
@@ -473,8 +456,6 @@
 
     for copy in started:
         copy.wait_send()
-    for copy in stores:
-        copy.wait()
 
 
 def on_device(
@@ -486,18 +467,18 @@
     vmem = pl.BlockSpec(memory_space=pltpu.VMEM)
     smem = pl.BlockSpec(memory_space=pltpu.SMEM)
     hbm = pl.BlockSpec(memory_space=pl.ANY)
-    copies = 3 + 8 + 7 + NCH * 15 + 7 + 3 + 7
+    copies = 6 + 16 + 7 + NCH * 12 + 7 + 3 + 7
     hidden_grad, router_grad, gate_grad, up_grad, down_grad = pl.pallas_call(
         functools.partial(kernel, D, F),
         out_shape=(
-            jax.ShapeDtypeStruct((TOK, D), BF16),
-            jax.ShapeDtypeStruct((1, D), F32),
-            jax.ShapeDtypeStruct((D, F), BF16),
-            jax.ShapeDtypeStruct((D, F), BF16),
-            jax.ShapeDtypeStruct((F, D), BF16),
+            pltpu.VMEM((TOK, D), BF16),
+            pltpu.VMEM((1, D), F32),
+            pltpu.VMEM((D, F), BF16),
+            pltpu.VMEM((D, F), BF16),
+            pltpu.VMEM((F, D), BF16),
         ),
         in_specs=[hbm, vmem, vmem, smem, vmem, hbm, hbm, hbm],
-        out_specs=(hbm, vmem, hbm, hbm, hbm),
+        out_specs=(vmem,)*5,
         scratch_shapes=[
             pltpu.VMEM((TOK, D), BF16),
             pltpu.VMEM((D, 2 * F), BF16),
@@ -507,9 +488,7 @@
             pltpu.VMEM((NCH, SLOT, C), BF16),
             pltpu.VMEM((NCH, SLOT, C), BF16),
             pltpu.VMEM((NCH, SLOT, C), BF16),
-            pltpu.VMEM((NCH, 2, OWN, C // 2), BF16),
-            pltpu.VMEM((NCH, 2, OWN, C), BF16),
-            pltpu.VMEM((NCH, 2, OWN, C // 2), BF16),
+            pltpu.VMEM((NCH, NY - 1, OWN, C), BF16),
             pltpu.VMEM((ROWS, C), BF16),
             pltpu.VMEM((NCH, 2, OWN, D + EXT), F32),
             pltpu.VMEM((NCH, 2, NX - 1, OWN, D + EXT), BF16),
@@ -521,10 +500,7 @@
             pltpu.VMEM((2 * NY - 1, 8, TOK), F32),
             pltpu.VMEM((NX, D // 128, 128), F32),
             pltpu.VMEM((NZ, D // 128, 128), F32),
-            pltpu.VMEM((TOK, D), BF16),
-            pltpu.VMEM((D, F), BF16),
-            pltpu.VMEM((D, F), BF16),
-            pltpu.VMEM((F, D), BF16),
+            pltpu.VMEM((TOK, 128), F32),
             pltpu.SemaphoreType.DMA((copies,)),
             pltpu.SemaphoreType.DMA((copies,)),
             pltpu.SemaphoreType.DMA((8,)),

time: 106 us -> 87.5 us (0.83)
  the two profiles are of different devices: /device:TPU:32 before, /device:TPU:8 now
where the time goes in v2:
time: 87.5 us; the launch traced here: 86.7 us
  Pallas kernels  81.1 us (93%)
  local copies, waits for them, and re-layouts  4.98 us (6%)
    pallas_call x1, Pallas kernels, on_device(): pl.pallas_call(functools.partial(kernel, D, F), out_shape=(pltpu.VMEM((TO...  81.1 us
    unnamed x5, local copies, waits for them, and re-layouts  4.98 us

profile of v2, /device:TPU:8, one launch (start us, length us, event | category | flops | bytes accessed | tf_op | source)
XLA Modules:
  0.0 86.7 jit_solution(9462657957433211807)
XLA Ops:
  0.6 81.1 %shard_map.119 = (bf16[128,1024]{1,0:T(8,128)(2,1)S(1)}, f32[1,1024]{1,0:T(1,128)S(1)}, bf16[1024,896]{1,0:T(8,128)(2,1)S(1)}, bf16[1024,896]{1,0:T(8,128)(2,1)S(1)}, bf16[896,1024]{1,0:T(8,128)(2,1)S(1)}) custom-call(bf16[128,1024]{1,0:T(8,128)(2,1)} %bitcast.6, f32[1,1024]{1,0:T(1,128)} %bitcast.7, f32[2,64]{1,0:T(2,128)} %teacher_ref.1, ...), custom_call_target="tpu_custom_call" | custom-call | tf_op jit(solution)/shard_map/pallas_call | solution.py:471
  81.7 0.7 copy.18
  82.4 0.6 copy.19
  83.0 1.2 %copy.20 = bf16[1024,896]{1,0:T(8,128)(2,1)} copy(bf16[1024,896]{1,0:T(8,128)(2,1)S(1)} %get-tuple-element.17) | data formatting | bytes 3670016
  84.2 1.2 %copy.21 = bf16[1024,896]{1,0:T(8,128)(2,1)} copy(bf16[1024,896]{1,0:T(8,128)(2,1)S(1)} %get-tuple-element.18) | data formatting | bytes 3670016
  85.5 1.2 %copy.22 = bf16[896,1024]{1,0:T(8,128)(2,1)} copy(bf16[896,1024]{1,0:T(8,128)(2,1)S(1)} %get-tuple-element.19) | data formatting | bytes 3670016

commit v3 on v2

--- a/solution.py
+++ b/solution.py
@@ -16,18 +16,20 @@
 OWN = 16
 ROWS = OWN * NX * NZ
 SLOT = OWN * NX
-CH = 2 * SLOT
-NCH = ROWS // CH
+CHUNKS = ((0,), (1, 2), (3, 4), (5, 6), (7,))
+NCH = len(CHUNKS)
+KEEPER = {0: 0, NCH - 1: 1}
 EXT = 128
 OFFSETS = (0, 1, -1, 2, -2, 3, -3, 4)
 
 ORDER = (
-    "GR:0", "GC:0", "T:0", "GR:1", "GC:1", "A:0", "GR:2", "B:0",
-    "GC:2", "A:1", "GR:3", "D:0", "B:1", "GC:3", "A:2", "B:2",
-    "A:3", "E:0", "D:1", "B:3", "F:0", "G:0", "D:2", "E:1",
-    "D:3", "H:0", "F:1", "E:2", "G:1", "E:3", "F:2", "G:2",
-    "F:3", "G:3", "H:1", "RX:0", "WI:0", "WI:1", "WI:2", "RZ:0",
-    "WI:3", "H:2", "WO:0", "WO:1", "WO:2", "WO:3", "H:3",
+    "GR:0", "GC:0", "A:0", "T:0", "B:0", "GR:1", "GC:1", "A:1",
+    "D:0", "B:1", "E:0", "GR:2", "GC:2", "A:2", "F:0", "D:1",
+    "B:2", "G:0", "GR:3", "GC:3", "A:3", "H:0", "E:1", "B:3",
+    "A:4", "D:2", "F:1", "B:4", "G:1", "D:3", "E:2", "D:4",
+    "H:1", "F:2", "E:4", "E:3", "G:2", "F:4", "F:3", "G:4",
+    "G:3", "RX:0", "H:2", "WI:0", "WI:1", "WI:2", "H:4", "RZ:0",
+    "WI:3", "WO:0", "WO:1", "WO:2", "WO:3", "H:3",
 )
 
 
@@ -118,10 +120,10 @@
     count = [0]
     started = []
 
-    def send(src, dst, device):
+    def make(src, dst, device):
         i = count[0]
         count[0] += 1
-        copy = pltpu.make_async_remote_copy(
+        return pltpu.make_async_remote_copy(
             src_ref=src,
             dst_ref=dst,
             send_sem=send_sem.at[i],
@@ -129,9 +131,18 @@
             device_id=device,
             device_id_type=MESH,
         )
+
+    def send(src, dst, device):
+        copy = make(src, dst, device)
         copy.start()
         started.append(copy)
         return copy
+
+    def on(core_of_chip, part):
+        if core_of_chip is None:
+            part()
+        else:
+            pl.when(core == core_of_chip)(part)
 
     lcount = [0]
 
@@ -191,6 +202,7 @@
     logit_col = jnp.sum(hid[...].astype(F32) * rw_ref[...], axis=1, keepdims=True)
     logit_row = jnp.sum(jnp.where(eye, logit_col, 0.0), axis=0, keepdims=True)
     lsend[...] = jnp.broadcast_to(logit_row, (8, TOK))
+    gx[1] = gather_x(1)
     lg = [send(lsend, lrecv.at[d - 1], at_n(d)) for d in range(1, 2 * NY)]
 
     gz = {}
@@ -207,8 +219,6 @@
             copy.wait_recv()
         if step == 0:
             gz[which, 1] = [ring(which, 0, 1, -1), ring(which, 0, 2, 1)]
-            if which == 0:
-                gx[1] = gather_x(1)
         elif step == 1:
             gz[which, 2] = [ring(which, 1, 3, -1), ring(which, 2, 4, 1)]
         elif step == 2:
@@ -225,8 +235,15 @@
     def block(j, base=0):
         return pl.ds(pl.multiple_of(base + lax.rem(y + j + NY, NY) * OWN, OWN), OWN)
 
+    def chunk(i):
+        base, rows = CHUNKS[i][0] * SLOT, len(CHUNKS[i]) * SLOT
+        keeper = KEEPER.get(i)
+        share = base if keeper is not None else base + core * SLOT
+        return keeper, base, rows, share
+
     def stage1(i):
-        rows = pl.ds(i * CH, CH)
+        keeper, base, n, _ = chunk(i)
+        rows = pl.ds(base, n)
         if i == 0:
             for copy in load_w:
                 copy.wait()
@@ -234,131 +251,151 @@
             for which in (0, 1):
                 for copy in gz[which, 4]:
                     copy.wait_recv()
-
-        for at, n in tiles(2 * F, 256):
-            cols = pl.ds(at, n)
-            part[i, :, cols] = jnp.dot(
+        for at, m in tiles(2 * F, 256):
+            cols = pl.ds(at, m)
+            part[rows, cols] = jnp.dot(
                 agb[0, rows, :], wgu[:, cols], preferred_element_type=F32
             )
-
-        for at, n in tiles(F, 256):
-            part[i, :, pl.ds(2 * F + at, n)] = nt(agb[1, rows, :], wd[pl.ds(at, n), :])
+        for at, m in tiles(F, 256):
+            part[rows, pl.ds(2 * F + at, m)] = nt(agb[1, rows, :], wd[pl.ds(at, m), :])
         logit = jnp.sum(agb[0, rows, :].astype(F32) * rw_ref[...], axis=1, keepdims=True)
-        part[i, :, pl.ds(3 * F, EXT)] = jnp.broadcast_to(logit, (CH, EXT))
-        other = pl.ds(pl.multiple_of((1 - core) * SLOT, SLOT), SLOT)
-        csend[i, :, pl.ds(0, 3 * F)] = part[i, other, pl.ds(0, 3 * F)].astype(BF16)
-        csend[i, :, pl.ds(3 * F, EXT)] = encode(
-            part[i, other, pl.ds(3 * F, EXT)][:, 0:1], SLOT
-        )
-        core_out[i] = send(csend.at[i], crecv.at[i], sibling)
+        part[rows, pl.ds(3 * F, EXT)] = jnp.broadcast_to(logit, (n, EXT))
+        if keeper is None:
+            other = pl.ds(pl.multiple_of(base + (1 - core) * SLOT, SLOT), SLOT)
+        else:
+            other = rows
+        copy = make(csend.at[i], crecv.at[i], sibling)
+        core_out[i] = copy
+
+        def to_other():
+            csend[i, :, pl.ds(0, 3 * F)] = part[other, pl.ds(0, 3 * F)].astype(BF16)
+            csend[i, :, pl.ds(3 * F, EXT)] = encode(
+                part[other, pl.ds(3 * F, EXT)][:, 0:1], SLOT
+            )
+            copy.start()
+
+        on(None if keeper is None else 1 - keeper, to_other)
 
     def stage2(i):
-        core_out[i].wait_recv()
-        base = pl.multiple_of(core * SLOT, SLOT)
-        mine = pl.ds(base, SLOT)
-        total = part[i, mine, pl.ds(0, 3 * F)] + crecv[i, :, pl.ds(0, 3 * F)].astype(F32)
-        part[i, mine, pl.ds(0, 3 * F)] = total
-        ysend[i, :, pl.ds(0, 3 * F)] = total.astype(BF16)
-        logit = part[i, mine, pl.ds(3 * F, EXT)][:, 0:1] + decode(
-            crecv[i, :, pl.ds(3 * F, EXT)]
-        )
-        part[i, mine, pl.ds(3 * F, EXT)] = jnp.broadcast_to(logit, (SLOT, EXT))
-        ysend[i, :, pl.ds(3 * F, EXT)] = encode(logit, SLOT)
-        y_out[i] = [
-            send(ysend.at[i, block(d)], yrecv.at[i, d - 1], at_y(d)) for d in (2, 1, 3)
+        keeper, _, _, share = chunk(i)
+        mine = pl.ds(share if keeper is not None else pl.multiple_of(share, SLOT), SLOT)
+        copies = [
+            make(ysend.at[i, block(d)], yrecv.at[i, d - 1], at_y(d)) for d in (2, 1, 3)
         ]
+        y_out[i] = copies
+
+        def add():
+            core_out[i].wait_recv()
+            total = part[mine, pl.ds(0, 3 * F)] + crecv[i, :, pl.ds(0, 3 * F)].astype(F32)
+            part[mine, pl.ds(0, 3 * F)] = total
+            ysend[i, :, pl.ds(0, 3 * F)] = total.astype(BF16)
+            logit = part[mine, pl.ds(3 * F, EXT)][:, 0:1] + decode(
+                crecv[i, :, pl.ds(3 * F, EXT)]
+            )
+            part[mine, pl.ds(3 * F, EXT)] = jnp.broadcast_to(logit, (SLOT, EXT))
+            ysend[i, :, pl.ds(3 * F, EXT)] = encode(logit, SLOT)
+            for copy in copies:
+                copy.start()
+
+        on(keeper, add)
 
     def stage4(i):
-        for copy in y_out[i]:
-            copy.wait_recv()
-        own = block(0, core * SLOT)
-
-        def total(at):
-            cols = pl.ds(at, F)
-            value = part[i, own, cols]
+        keeper, _, _, share = chunk(i)
+        own = block(0, share)
+        ext = pl.ds(3 * F, EXT)
+        copies = [make(gact.at[own], gact.at[own], at_y(d)) for d in (1, -1)]
+        g_first[i] = copies
+
+        def gate_block():
+            for copy in y_out[i]:
+                copy.wait_recv()
+
+            def total(at):
+                cols = pl.ds(at, F)
+                value = part[own, cols]
+                for d in range(NY - 1):
+                    value = value + yrecv[i, d, :, cols].astype(F32)
+                return value
+
+            logit = part[own, ext][:, 0:1]
             for d in range(NY - 1):
-                value = value + yrecv[i, d, :, cols].astype(F32)
-            return value
-
-        ext = pl.ds(3 * F, EXT)
-        logit = part[i, own, ext][:, 0:1]
-        for d in range(NY - 1):
-            logit = logit + decode(yrecv[i, d, :, ext])
-        scale = jax.nn.sigmoid(logit)
-        gate, up, raw = total(0), total(F), total(2 * F)
-        sig = jax.nn.sigmoid(gate)
-        silu = gate * sig
-        act = silu * up
-        act_grad = scale * raw
-        out = block(0, i * CH + core * SLOT)
-        gact[out, pl.ds(0, F)] = (act_grad * up * sig * (1.0 + gate * (1.0 - sig))).astype(BF16)
-        gact[out, pl.ds(F, F)] = (act_grad * silu).astype(BF16)
-        gact[out, pl.ds(2 * F, F)] = (scale * act).astype(BF16)
-        dots = jnp.sum(act * raw, axis=1, keepdims=True)
-        gact[out, ext] = encode(scale * (1.0 - scale) * dots, OWN)
-        g_first[i] = [
-            send(gact.at[out], gact.at[out], at_y(1)),
-            send(gact.at[out], gact.at[out], at_y(-1)),
-        ]
+                logit = logit + decode(yrecv[i, d, :, ext])
+            scale = jax.nn.sigmoid(logit)
+            gate, up, raw = total(0), total(F), total(2 * F)
+            sig = jax.nn.sigmoid(gate)
+            silu = gate * sig
+            act = silu * up
+            act_grad = scale * raw
+            gate_pre = act_grad * up * sig * (1.0 + gate * (1.0 - sig))
+            gact[own, pl.ds(0, F)] = gate_pre.astype(BF16)
+            gact[own, pl.ds(F, F)] = (act_grad * silu).astype(BF16)
+            gact[own, pl.ds(2 * F, F)] = (scale * act).astype(BF16)
+            dots = jnp.sum(act * raw, axis=1, keepdims=True)
+            gact[own, ext] = encode(scale * (1.0 - scale) * dots, OWN)
+            for copy in copies:
+                copy.start()
+
+        on(keeper, gate_block)
 
     def stage5(i):
-        base = i * CH + core * SLOT
-        g_first[i][0].wait_recv()
-        left = gact.at[block(-1, base), pl.ds(0, H)]
-        a = send(left, left, at_y(1))
-        g_first[i][1].wait_recv()
-        right = gact.at[block(1, base), pl.ds(H, H)]
-        b = send(right, right, at_y(-1))
-        g_second[i] = [a, b]
+        keeper, _, _, share = chunk(i)
+        left = gact.at[block(-1, share), pl.ds(0, H)]
+        right = gact.at[block(1, share), pl.ds(H, H)]
+        copies = [make(left, left, at_y(1)), make(right, right, at_y(-1))]
+        g_second[i] = copies
+
+        def hand_on():
+            for first, second in zip(g_first[i], copies):
+                first.wait_recv()
+                second.start()
+
+        on(keeper, hand_on)
 
     def stage6(i):
-        for copy in g_second[i]:
-            copy.wait_recv()
-        half = gact.at[pl.ds(pl.multiple_of(i * CH + core * SLOT, SLOT), SLOT)]
-        core_back[i] = send(half, half, sibling)
+        keeper, _, _, share = chunk(i)
+        start = share if keeper is not None else pl.multiple_of(share, SLOT)
+        half = gact.at[pl.ds(start, SLOT)]
+        copy = make(half, half, sibling)
+        core_back[i] = copy
+
+        def give():
+            for second in g_second[i]:
+                second.wait_recv()
+            copy.start()
+
+        on(keeper, give)
 
     def stage7(i):
-        core_back[i].wait_recv()
-        rows = pl.ds(i * CH, CH)
-
-        for at, n in tiles(D, 256):
-            cols = pl.ds(at, n)
-            out = nt(gact[rows, pl.ds(0, 2 * F)], wgu[cols, :])
-            for s in range(2):
+        keeper, base, n, _ = chunk(i)
+        on(None if keeper is None else 1 - keeper, core_back[i].wait_recv)
+        rows = pl.ds(base, n)
+        routed = decode(gact[rows, pl.ds(3 * F, EXT)])
+        for at, m in tiles(D, 256):
+            cols = pl.ds(at, m)
+            out = nt(gact[rows, pl.ds(0, 2 * F)], wgu[cols, :]) + routed * rw_ref[:, cols]
+            for s, k in enumerate(CHUNKS[i]):
                 for j in range(NX):
                     piece = out[s * SLOT + j * OWN : s * SLOT + (j + 1) * OWN]
                     if j == 0:
-                        rgf[i, s, :, cols] = piece
+                        rgf[k, :, cols] = piece
                     else:
-                        xsend[i, s, j - 1, :, cols] = piece.astype(BF16)
-
-        for s in range(2):
-            for j in range(NX):
-                ext = gact[pl.ds(i * CH + s * SLOT + j * OWN, OWN), pl.ds(3 * F, EXT)]
-                if j == 0:
-                    rgf[i, s, :, pl.ds(D, EXT)] = jnp.broadcast_to(decode(ext), (OWN, EXT))
-                else:
-                    xsend[i, s, j - 1, :, pl.ds(D, EXT)] = ext
+                        xsend[k, j - 1, :, cols] = piece.astype(BF16)
+        slots = pl.ds(CHUNKS[i][0], len(CHUNKS[i]))
         x_out[i] = [
-            send(xsend.at[i, :, j - 1], xrecv.at[i, j - 1], at_x(j)) for j in (2, 1, 3)
+            send(xsend.at[slots, j - 1], xrecv.at[slots, j - 1], at_x(j)) for j in (2, 1, 3)
         ]
 
     def stage8(i):
         for copy in x_out[i]:
             copy.wait_recv()
-        for s in range(2):
-            k = 2 * i + s
-            total = rgf[i, s, :, pl.ds(0, D)]
-            extra = rgf[i, s, :, pl.ds(D, EXT)][:, 0:1]
+        for k in CHUNKS[i]:
+            total = rgf[k]
             for j in range(NX - 1):
-                total = total + xrecv[i, j, s, :, pl.ds(0, D)].astype(F32)
-                extra = extra + decode(xrecv[i, j, s, :, pl.ds(D, EXT)])
+                total = total + xrecv[k, j].astype(F32)
             if k == 0:
-                zown[:, pl.ds(0, D)] = total
-                zown[:, pl.ds(D, EXT)] = jnp.broadcast_to(extra, (OWN, EXT))
+                zown[...] = total
             else:
-                zsend[k - 1, :, pl.ds(0, D)] = total.astype(BF16)
-                zsend[k - 1, :, pl.ds(D, EXT)] = encode(extra, OWN)
+                zsend[k - 1] = total.astype(BF16)
                 z_out[k] = send(zsend.at[k - 1], zrecv.at[k - 1], at_z(OFFSETS[k]))
 
     held = {}
@@ -429,14 +466,26 @@
         name, step = task.split(":")
         tasks[name](int(step))
 
+    late = list(z_out.values()) + held["rz"]
+    late_ids = [id(copy) for copy in late]
+    for copy in started:
+        if id(copy) not in late_ids:
+            copy.wait_send()
+    for i in range(NCH):
+        keeper = KEEPER.get(i)
+
+        def sent(keeper=keeper, i=i):
+            for copy in y_out[i] + g_first[i] + g_second[i] + [core_back[i]]:
+                copy.wait_send()
+
+        on(keeper, sent)
+        on(None if keeper is None else 1 - keeper, core_out[i].wait_send)
+
     for k in range(1, NZ):
         z_out[k].wait_recv()
-    total = zown[:, pl.ds(0, D)]
-    extra = zown[:, pl.ds(D, EXT)][:, 0:1]
+    total = zown[...]
     for k in range(NZ - 1):
-        total = total + zrecv[k, :, pl.ds(0, D)].astype(F32)
-        extra = extra + decode(zrecv[k, :, pl.ds(D, EXT)])
-    total = total + extra * rw_ref[...]
+        total = total + zrecv[k].astype(F32)
     high = total.astype(BF16)
     low = (total - high.astype(F32)).astype(BF16)
     place16 = place.astype(BF16)
@@ -454,7 +503,7 @@
     for a in range(D // 128):
         rg_ref[:, a * 128 : (a + 1) * 128] = final[a : a + 1, :]
 
-    for copy in started:
+    for copy in late:
         copy.wait_send()
 
 
@@ -484,18 +533,18 @@
             pltpu.VMEM((D, 2 * F), BF16),
             pltpu.VMEM((F, D), BF16),
             pltpu.VMEM((2, ROWS, D), BF16),
-            pltpu.VMEM((NCH, CH, C), F32),
+            pltpu.VMEM((ROWS, C), F32),
             pltpu.VMEM((NCH, SLOT, C), BF16),
             pltpu.VMEM((NCH, SLOT, C), BF16),
             pltpu.VMEM((NCH, SLOT, C), BF16),
             pltpu.VMEM((NCH, NY - 1, OWN, C), BF16),
             pltpu.VMEM((ROWS, C), BF16),
-            pltpu.VMEM((NCH, 2, OWN, D + EXT), F32),
-            pltpu.VMEM((NCH, 2, NX - 1, OWN, D + EXT), BF16),
-            pltpu.VMEM((NCH, NX - 1, 2, OWN, D + EXT), BF16),
-            pltpu.VMEM((OWN, D + EXT), F32),
-            pltpu.VMEM((NZ - 1, OWN, D + EXT), BF16),
-            pltpu.VMEM((NZ - 1, OWN, D + EXT), BF16),
+            pltpu.VMEM((NZ, OWN, D), F32),
+            pltpu.VMEM((NZ, NX - 1, OWN, D), BF16),
+            pltpu.VMEM((NZ, NX - 1, OWN, D), BF16),
+            pltpu.VMEM((OWN, D), F32),
+            pltpu.VMEM((NZ - 1, OWN, D), BF16),
+            pltpu.VMEM((NZ - 1, OWN, D), BF16),
             pltpu.VMEM((8, TOK), F32),
             pltpu.VMEM((2 * NY - 1, 8, TOK), F32),
             pltpu.VMEM((NX, D // 128, 128), F32),

time: 87.5 us -> 80 us (0.914)
  Pallas kernels: 81.1 us -> 74.2 us
    pallas_call x1, Pallas kernels: 81.1 us -> 74.2 us  [on_device(): pl.pallas_call(functools.partial(kernel, D, F), out_shape=(pltpu.VMEM((TO...]
where the time goes in v3:
time: 80 us; the launch traced here: 79.8 us
  Pallas kernels  74.2 us (93%)
  local copies, waits for them, and re-layouts  4.98 us (6%)
    pallas_call x1, Pallas kernels, on_device(): pl.pallas_call(functools.partial(kernel, D, F), out_shape=(pltpu.VMEM((TO...  74.2 us
    unnamed x5, local copies, waits for them, and re-layouts  4.98 us

profile of v3, /device:TPU:8, one launch (start us, length us, event | category | flops | bytes accessed | tf_op | source)
XLA Modules:
  0.0 79.8 jit_solution(2481934421176665446)
XLA Ops:
  0.6 74.2 %shard_map.119 = (bf16[128,1024]{1,0:T(8,128)(2,1)S(1)}, f32[1,1024]{1,0:T(1,128)S(1)}, bf16[1024,896]{1,0:T(8,128)(2,1)S(1)}, bf16[1024,896]{1,0:T(8,128)(2,1)S(1)}, bf16[896,1024]{1,0:T(8,128)(2,1)S(1)}) custom-call(bf16[128,1024]{1,0:T(8,128)(2,1)} %bitcast.6, f32[1,1024]{1,0:T(1,128)} %bitcast.7, f32[2,64]{1,0:T(2,128)} %teacher_ref.1, ...), custom_call_target="tpu_custom_call" | custom-call | tf_op jit(solution)/shard_map/pallas_call | solution.py:520
  74.8 0.7 copy.18
  75.5 0.6 copy.19
  76.1 1.2 %copy.20 = bf16[1024,896]{1,0:T(8,128)(2,1)} copy(bf16[1024,896]{1,0:T(8,128)(2,1)S(1)} %get-tuple-element.17) | data formatting | bytes 3670016
  77.3 1.2 %copy.21 = bf16[1024,896]{1,0:T(8,128)(2,1)} copy(bf16[1024,896]{1,0:T(8,128)(2,1)S(1)} %get-tuple-element.18) | data formatting | bytes 3670016
  78.6 1.2 %copy.22 = bf16[896,1024]{1,0:T(8,128)(2,1)} copy(bf16[896,1024]{1,0:T(8,128)(2,1)S(1)} %get-tuple-element.19) | data formatting | bytes 3670016

commit v4 on v3

--- a/solution.py
+++ b/solution.py
@@ -505,6 +505,28 @@
 
     for copy in late:
         copy.wait_send()
+
+
+def store_kernel(*refs):
+    n = len(refs) // 2
+    sems = refs[-1]
+    copies = [pltpu.make_async_copy(refs[i], refs[n + i], sems.at[i]) for i in range(n)]
+    for copy in copies:
+        copy.start()
+    for copy in copies:
+        copy.wait()
+
+
+def store(arrays):
+    arrays = [pltpu.with_memory_space_constraint(a, pltpu.VMEM) for a in arrays]
+    return pl.pallas_call(
+        store_kernel,
+        out_shape=tuple(jax.ShapeDtypeStruct(a.shape, a.dtype) for a in arrays),
+        in_specs=[pl.BlockSpec(memory_space=pltpu.VMEM)] * len(arrays),
+        out_specs=(pl.BlockSpec(memory_space=pl.ANY),) * len(arrays),
+        scratch_shapes=[pltpu.SemaphoreType.DMA((len(arrays),))],
+        compiler_params=pltpu.CompilerParams(vmem_limit_bytes=8 * 1024 * 1024),
+    )(*arrays)
 
 
 def on_device(
@@ -569,6 +591,9 @@
         up_weight,
         down_weight,
     )
+    hidden_grad, router_grad, gate_grad, up_grad, down_grad = store(
+        (hidden_grad, router_grad, gate_grad, up_grad, down_grad)
+    )
     return (
         hidden_grad.reshape(hidden.shape),
         router_grad.reshape(D),

time: 80 us -> 77.8 us (0.972)
  local copies, waits for them, and re-layouts: 4.98 us -> 0 us
  Pallas kernels: 74.2 us -> 76.7 us
    unnamed x5 -> x0, local copies, waits for them, and re-layouts: 4.98 us -> none
    pallas_call x0 -> x1, Pallas kernels: none -> 2.57 us  [store(): pl.pallas_call(store_kernel, out_shape=tuple((jax.ShapeDtypeStruct(a.shap...]
where the time goes in v4:
time: 77.8 us; the launch traced here: 77.5 us
  Pallas kernels  76.7 us (99%)
  between operations  0.8 us (1%)
    pallas_call x1, Pallas kernels, on_device(): pl.pallas_call(functools.partial(kernel, D, F), out_shape=(pltpu.VMEM((TO...  74.2 us
    pallas_call x1, Pallas kernels, store(): pl.pallas_call(store_kernel, out_shape=tuple((jax.ShapeDtypeStruct(a.shap...  2.57 us

profile of v4, /device:TPU:8, one launch (start us, length us, event | category | flops | bytes accessed | tf_op | source)
XLA Modules:
  0.0 77.5 jit_solution(16828310857623401211)
XLA Ops:
  0.6 74.2 %shard_map.119 = (bf16[128,1024]{1,0:T(8,128)(2,1)S(1)}, f32[1,1024]{1,0:T(1,128)S(1)}, bf16[1024,896]{1,0:T(8,128)(2,1)S(1)}, bf16[1024,896]{1,0:T(8,128)(2,1)S(1)}, bf16[896,1024]{1,0:T(8,128)(2,1)S(1)}) custom-call(bf16[128,1024]{1,0:T(8,128)(2,1)} %bitcast.4, f32[1,1024]{1,0:T(1,128)} %bitcast.5, f32[2,64]{1,0:T(2,128)} %teacher_ref.1, ...), custom_call_target="tpu_custom_call" | custom-call | tf_op jit(solution)/shard_map/pallas_call | solution.py:542
  74.8 2.6 %shard_map.120 = (bf16[128,1024]{1,0:T(8,128)(2,1)}, f32[1,1024]{1,0:T(1,128)}, bf16[1024,896]{1,0:T(8,128)(2,1)}, bf16[1024,896]{1,0:T(8,128)(2,1)}, bf16[896,1024]{1,0:T(8,128)(2,1)}) custom-call(bf16[128,1024]{1,0:T(8,128)(2,1)S(1)} %get-tuple-element.15.refs_0_, f32[1,1024]{1,0:T(1,128)S(1)} %get-tuple-element.16.refs_1_, ...), custom_call_target="tpu_custom_call" | custom-call | tf_op jit(solution)/shard_map/pallas_call | solution.py:522

commit v5 on v4

--- a/solution.py
+++ b/solution.py
@@ -24,12 +24,12 @@
 
 ORDER = (
     "GR:0", "GC:0", "A:0", "T:0", "B:0", "GR:1", "GC:1", "A:1",
-    "D:0", "B:1", "E:0", "GR:2", "GC:2", "A:2", "F:0", "D:1",
-    "B:2", "G:0", "GR:3", "GC:3", "A:3", "H:0", "E:1", "B:3",
-    "A:4", "D:2", "F:1", "B:4", "G:1", "D:3", "E:2", "D:4",
-    "H:1", "F:2", "E:4", "E:3", "G:2", "F:4", "F:3", "G:4",
-    "G:3", "RX:0", "H:2", "WI:0", "WI:1", "WI:2", "H:4", "RZ:0",
-    "WI:3", "WO:0", "WO:1", "WO:2", "WO:3", "H:3",
+    "D:0", "GR:2", "B:1", "E:0", "GC:2", "A:2", "GR:3", "B:2",
+    "D:1", "F:0", "GC:3", "A:3", "G:0", "B:3", "A:4", "D:2",
+    "H:0", "E:1", "B:4", "D:3", "E:2", "F:1", "D:4", "G:1",
+    "E:3", "F:2", "E:4", "G:2", "F:3", "F:4", "H:1", "G:3",
+    "G:4", "RX:0", "WI:0", "H:2", "WI:1", "WI:2", "WI:3", "WO:0",
+    "WO:1", "H:3", "WO:2", "WO:3", "H:4", "RZ:0",
 )
 
 

time: 77.8 us -> 75.9 us (0.976)
  Pallas kernels: 76.7 us -> 75 us
    pallas_call x1, Pallas kernels: 74.2 us -> 72.4 us  [on_device(): pl.pallas_call(functools.partial(kernel, D, F), out_shape=(pltpu.VMEM((TO...]
where the time goes in v5:
time: 75.9 us; the launch traced here: 75.8 us
  Pallas kernels  75 us (99%)
  between operations  0.8 us (1%)
    pallas_call x1, Pallas kernels, on_device(): pl.pallas_call(functools.partial(kernel, D, F), out_shape=(pltpu.VMEM((TO...  72.4 us
    pallas_call x1, Pallas kernels, store(): pl.pallas_call(store_kernel, out_shape=tuple((jax.ShapeDtypeStruct(a.shap...  2.57 us

profile of v5, /device:TPU:8, one launch (start us, length us, event | category | flops | bytes accessed | tf_op | source)
XLA Modules:
  0.0 75.8 jit_solution(10045679676279429645)
XLA Ops:
  0.6 72.4 %shard_map.119 = (bf16[128,1024]{1,0:T(8,128)(2,1)S(1)}, f32[1,1024]{1,0:T(1,128)S(1)}, bf16[1024,896]{1,0:T(8,128)(2,1)S(1)}, bf16[1024,896]{1,0:T(8,128)(2,1)S(1)}, bf16[896,1024]{1,0:T(8,128)(2,1)S(1)}) custom-call(bf16[128,1024]{1,0:T(8,128)(2,1)} %bitcast.4, f32[1,1024]{1,0:T(1,128)} %bitcast.5, f32[2,64]{1,0:T(2,128)} %teacher_ref.1, ...), custom_call_target="tpu_custom_call" | custom-call | tf_op jit(solution)/shard_map/pallas_call | solution.py:542
  73.1 2.6 %shard_map.120 = (bf16[128,1024]{1,0:T(8,128)(2,1)}, f32[1,1024]{1,0:T(1,128)}, bf16[1024,896]{1,0:T(8,128)(2,1)}, bf16[1024,896]{1,0:T(8,128)(2,1)}, bf16[896,1024]{1,0:T(8,128)(2,1)}) custom-call(bf16[128,1024]{1,0:T(8,128)(2,1)S(1)} %get-tuple-element.15.refs_0_, f32[1,1024]{1,0:T(1,128)S(1)} %get-tuple-element.16.refs_1_, ...), custom_call_target="tpu_custom_call" | custom-call | tf_op jit(solution)/shard_map/pallas_call | solution.py:522

commit v6 on v5

--- a/solution.py
+++ b/solution.py
@@ -29,7 +29,7 @@
     "H:0", "E:1", "B:4", "D:3", "E:2", "F:1", "D:4", "G:1",
     "E:3", "F:2", "E:4", "G:2", "F:3", "F:4", "H:1", "G:3",
     "G:4", "RX:0", "WI:0", "H:2", "WI:1", "WI:2", "WI:3", "WO:0",
-    "WO:1", "H:3", "WO:2", "WO:3", "H:4", "RZ:0",
+    "WO:1", "H:3", "H:4", "RZ:0", "WO:2", "WO:3",
 )
 
 

time: 75.9 us -> 75.9 us (level)
  no operation moved by 1% of the time
where the time goes in v6:
time: 75.9 us; the launch traced here: 75.8 us
  Pallas kernels  75 us (99%)
  between operations  0.8 us (1%)
    pallas_call x1, Pallas kernels, on_device(): pl.pallas_call(functools.partial(kernel, D, F), out_shape=(pltpu.VMEM((TO...  72.4 us
    pallas_call x1, Pallas kernels, store(): pl.pallas_call(store_kernel, out_shape=tuple((jax.ShapeDtypeStruct(a.shap...  2.57 us

profile of v6, /device:TPU:8, one launch (start us, length us, event | category | flops | bytes accessed | tf_op | source)
XLA Modules:
  0.0 75.8 jit_solution(11300662197254739280)
XLA Ops:
  0.6 72.4 %shard_map.119 = (bf16[128,1024]{1,0:T(8,128)(2,1)S(1)}, f32[1,1024]{1,0:T(1,128)S(1)}, bf16[1024,896]{1,0:T(8,128)(2,1)S(1)}, bf16[1024,896]{1,0:T(8,128)(2,1)S(1)}, bf16[896,1024]{1,0:T(8,128)(2,1)S(1)}) custom-call(bf16[128,1024]{1,0:T(8,128)(2,1)} %bitcast.4, f32[1,1024]{1,0:T(1,128)} %bitcast.5, f32[2,64]{1,0:T(2,128)} %teacher_ref.1, ...), custom_call_target="tpu_custom_call" | custom-call | tf_op jit(solution)/shard_map/pallas_call | solution.py:542
  73.1 2.6 %shard_map.120 = (bf16[128,1024]{1,0:T(8,128)(2,1)}, f32[1,1024]{1,0:T(1,128)}, bf16[1024,896]{1,0:T(8,128)(2,1)}, bf16[1024,896]{1,0:T(8,128)(2,1)}, bf16[896,1024]{1,0:T(8,128)(2,1)}) custom-call(bf16[128,1024]{1,0:T(8,128)(2,1)S(1)} %get-tuple-element.15.refs_0_, f32[1,1024]{1,0:T(1,128)S(1)} %get-tuple-element.16.refs_1_, ...), custom_call_target="tpu_custom_call" | custom-call | tf_op jit(solution)/shard_map/pallas_call | solution.py:522
